TPU v7x, 256 devices: a whole 4x4x8 slice. The times are simulated.
256 devices in a mesh: bag: 32 (over x, z), head: 8 (over y, core).
Axes of the slice: x: 4, y: 4, z: 8, core: 2. Of those that a mesh axis runs over, the one named last changes fastest.
Arguments:
- latents: bfloat16 [32, 16, 16, 16, 512], P('bag', 'head'), may hold values from -6 to 6
- frame_counts: int32 [32], P('bag'), may hold values from 8 to 16
- routes: int32 [32768, 1], P('bag'), may hold values from 0 to 31; in each aligned block of 128 rows (0 to 127, 128 to 255, ...) at most 6 rows name the same one
- samples: int32 [32768], P('bag'), may hold values from 0 to 3, as said below
- conv_weight: bfloat16 [27, 512, 128], replicated, may hold values from -0.0546875 to 0.0546875
- embed_weight: bfloat16 [512, 2048], replicated, may hold values from -0.25 to 0.25
- qkv_weight: bfloat16 [3, 2048, 2048], P(None, None, 'head')
Outputs:
- attended: bfloat16 [32768, 2048], P(('bag', 'head'))
Inputs may be any that keep to these rules, and one draw needn't show every extreme that they name: `routes`: in each aligned block of 128 rows (the tokens of one device) no bag is named by more than 6 rows, a bound that some block reaches. `samples`: all tokens of one clip carry the same sample id, and every id occurs in some clip.
All inputs are finite; a program needn't handle non-finite values.
Results may differ from a plain program's by a relative error of at most 0.013.
Values may be sent and summed in bfloat16 or wider, within the bound.
A program may use at most 128 MiB of HBM per device.

v0:
```python
import jax
import jax.numpy as jnp
from jax import lax
from jax.experimental import pallas as pl
from jax.experimental.pallas import tpu as pltpu
from jax.sharding import PartitionSpec as P

BAGS = 32
HEAD_DEVS = 8
CORES = 2
TOK = 128
CAP = 6
MSG = 32
ROWS = BAGS * CAP
SLOTS = HEAD_DEVS * ROWS
PER_BAG = HEAD_DEVS * CAP
FRAMES_DEV = 2
CELLS = 256
CIN = 512
COUT = 128
D = 2048
WIDTH = 256
HDIM = 64
GROUPS = 4
GROUP_CLIPS = BAGS // GROUPS
PIECE = GROUP_CLIPS * CAP
GROUP = HEAD_DEVS * PIECE
ALIGN = 128
QTILE = 384
KTILE = 384
SORTED = SLOTS + 4 * ALIGN + KTILE
epsilon = 1e-06
far_below = -1e30

MESH = pl.DeviceIdType.MESH
bf16 = jnp.bfloat16
f32 = jnp.float32
i32 = jnp.int32


def iota(shape, dim):
    return lax.broadcasted_iota(i32, shape, dim)


def dot(a, b):
    return jnp.dot(a, b, preferred_element_type=f32)


def greet(bag, head):
    barrier = pltpu.get_barrier_semaphore()

    def along_bag(step, carry):
        pl.semaphore_signal(
            barrier, inc=1, device_id=(lax.rem(bag + step, BAGS), head), device_id_type=MESH
        )
        return carry

    def along_head(step, carry):
        pl.semaphore_signal(
            barrier, inc=1, device_id=(bag, lax.rem(head + step, HEAD_DEVS)), device_id_type=MESH
        )
        return carry

    lax.fori_loop(1, HEAD_DEVS, along_head, 0)
    lax.fori_loop(1, BAGS, along_bag, 0)


def met():
    pl.semaphore_wait(pltpu.get_barrier_semaphore(), BAGS + HEAD_DEVS - 2)


def front_kernel(
    count_ref,
    routes_ref,
    samples_ref,
    latents_ref,
    conv_ref,
    embed_ref,
    qkv_ref,
    q_out,
    k_out,
    v_out,
    plan_ref,
    valid_ref,
    taps,
    frames,
    sums,
    edge_out,
    edge_in,
    grid,
    scatter,
    outbox,
    inbox,
    unpack,
    rows,
    embed,
    qkv,
    normed,
    targets,
    q_ref,
    k_ref,
    v_ref,
    load_sem,
    tap_sem,
    halo_send,
    halo_recv,
    bag_send,
    bag_recv,
    local_sem,
    head_send,
    head_recv,
    store_sem,
):
    bag = lax.axis_index("bag")
    head = lax.axis_index("head")
    core = lax.rem(head, CORES)
    chip = lax.div(head, CORES)
    count = count_ref[0]

    loads = [
        pltpu.make_async_copy(latents_ref.at[f], frames.at[f], load_sem.at[f])
        for f in range(FRAMES_DEV)
    ]
    for load in loads:
        load.start()
    for a in (2, 0, 1):
        for be in range(9):
            pltpu.make_async_copy(
                conv_ref.at[9 * a + be], taps.at[a, :, pl.ds(be * COUT, COUT)], tap_sem.at[a]
            ).start()

    weights = [
        pltpu.make_async_copy(embed_ref, embed, load_sem.at[2]),
        pltpu.make_async_copy(qkv_ref, qkv, load_sem.at[3]),
    ]
    for load in weights:
        load.start()

    edge_in[...] = jnp.zeros_like(edge_in)
    greet(bag, head)

    def taps_here(a):
        pltpu.make_async_copy(taps.at[a], taps.at[a], tap_sem.at[a]).wait()

    def add_taps(slot, a, out):
        scale = jnp.where(head * FRAMES_DEV + slot < count, 1.0, 0.0)
        cells = (frames[slot].astype(f32) * scale).astype(bf16)
        made = dot(cells, taps[a])
        for e in range(3):
            sums[out, e] += made[:, (3 + e) * COUT : (4 + e) * COUT]
            sums[out, e, 16:CELLS] += made[: CELLS - 16, e * COUT : (e + 1) * COUT]
            sums[out, e, : CELLS - 16] += made[16:, (6 + e) * COUT : (7 + e) * COUT]

    column = lax.rem(iota((CELLS, COUT), 0), 16)

    def joined(out):
        from_left = jnp.where(column == 0, 0.0, pltpu.roll(sums[out, 0], 1, 0))
        from_right = jnp.where(column == 15, 0.0, pltpu.roll(sums[out, 2], CELLS - 1, 0))
        return sums[out, 1] + from_left + from_right

    sums[...] = jnp.zeros_like(sums)
    loads[0].wait()
    taps_here(2)
    add_taps(0, 2, 2)
    edge_out[1] = joined(2).astype(bf16)
    loads[1].wait()
    taps_here(0)
    add_taps(1, 0, 3)
    edge_out[0] = joined(3).astype(bf16)
    met()

    def edge(side, to):
        return pltpu.make_async_remote_copy(
            src_ref=edge_out.at[side],
            dst_ref=edge_in.at[side],
            send_sem=halo_send.at[side],
            recv_sem=halo_recv.at[side],
            device_id=(bag, to),
            device_id_type=MESH,
        )

    to_right = edge(0, lax.rem(head + 1, HEAD_DEVS))
    to_left = edge(1, lax.rem(head + HEAD_DEVS - 1, HEAD_DEVS))

    @pl.when(head < HEAD_DEVS - 1)
    def _():
        to_right.start()

    @pl.when(head > 0)
    def _():
        to_left.start()

    lane = iota((1, TOK), 1)
    bag_row = iota((BAGS, TOK), 0)
    half = (lane >= TOK // 2).astype(i32)
    lanes32 = iota((BAGS, TOK), 1)
    meta = jnp.where(lanes32 == HEAD_DEVS, samples_ref[0:1, 0:1].astype(f32), 0.0)
    for h in range(HEAD_DEVS):
        named = (routes_ref[h : h + 1, :] == bag_row) & (h * FRAMES_DEV + half < count)
        per_bag = jnp.sum(named.astype(f32), axis=1, keepdims=True)
        meta = meta + jnp.where(lanes32 == h, per_bag, 0.0)
    route = routes_ref[pl.ds(head, 1), :]
    live = head * FRAMES_DEV + half < count
    named = ((route == bag_row) & live).astype(f32)
    before = (iota((TOK, TOK), 0) < iota((TOK, TOK), 1)).astype(bf16)
    rank = jnp.sum(named * dot(named.astype(bf16), before), axis=0, keepdims=True)
    target = jnp.where(live, route * MSG + rank.astype(i32), -1000)
    out_row = iota((BAGS * MSG, TOK), 0)
    for q in range(4):
        scatter[:, q * TOK : (q + 1) * TOK] = (out_row == target + CAP * q).astype(f32).astype(bf16)

    add_taps(0, 0, 1)
    add_taps(1, 2, 0)
    taps_here(1)
    add_taps(0, 1, 0)
    add_taps(1, 1, 1)

    @pl.when(head > 0)
    def _():
        to_right.wait_recv()

    @pl.when(head < HEAD_DEVS - 1)
    def _():
        to_left.wait_recv()

    for f in range(FRAMES_DEV):
        scale = jnp.where(head * FRAMES_DEV + f < count, 1.0, 0.0)
        total = (joined(f) + edge_in[f].astype(f32)) * scale
        grid[f * 16 : (f + 1) * 16] = total.reshape(16, 16, COUT)
    quarters = []
    for di in range(2):
        for dj in range(2):
            quarters.extend(grid[2 * r + di, pl.ds(dj, 8, stride=2), :] for r in range(16))
    patches = jnp.concatenate(quarters, axis=0).astype(bf16)

    meta_here = (iota((BAGS * MSG, BAGS), 0) == iota((BAGS * MSG, BAGS), 1) * MSG + 4 * CAP).astype(f32)
    outbox[...] = (dot(scatter[...], patches) + dot(meta_here.astype(bf16), meta.astype(bf16))).astype(bf16)

    def message(ref, at):
        return ref.at[pl.ds(pl.multiple_of(at * MSG, MSG), MSG)]

    own = pltpu.make_async_copy(message(outbox, bag), message(inbox, bag), local_sem.at[0])
    own.start()

    def send(step, carry):
        to = lax.rem(bag + step, BAGS)
        pltpu.make_async_remote_copy(
            src_ref=message(outbox, to),
            dst_ref=message(inbox, bag),
            send_sem=bag_send,
            recv_sem=bag_recv,
            device_id=(to, head),
            device_id_type=MESH,
        ).start()
        return carry

    lax.fori_loop(1, BAGS, send, 0)

    slot = iota((ROWS, BAGS * MSG), 0)
    clip_of = lax.shift_right_logical(slot * 10923, 16)
    wanted = clip_of * MSG + (slot - clip_of * CAP)
    at_col = iota((ROWS, BAGS * MSG), 1)
    for q in range(4):
        unpack[q * ROWS : (q + 1) * ROWS] = (at_col == wanted + q * CAP).astype(f32).astype(bf16)

    own.wait()
    others = inbox.at[pl.ds(0, (BAGS - 1) * MSG)]
    pltpu.make_async_copy(others, others, bag_recv).wait()

    def piece(of, group):
        return rows.at[pl.ds(pl.multiple_of(group * GROUP + of * PIECE, PIECE), PIECE)]

    unpacked = dot(unpack[...], inbox[...]).astype(bf16)
    for g in range(GROUPS):
        at = pl.ds(pl.multiple_of(g * GROUP + head * PIECE, PIECE), PIECE)
        for q in range(4):
            first_row = q * ROWS + g * PIECE
            rows[at, q * COUT : (q + 1) * COUT] = unpacked[first_row : first_row + PIECE]

    sibling = chip * CORES + 1 - core

    def push(of, group, to, sem):
        return pltpu.make_async_remote_copy(
            src_ref=piece(of, group),
            dst_ref=piece(of, group),
            send_sem=head_send.at[sem],
            recv_sem=head_recv.at[group, of],
            device_id=(bag, to),
            device_id_type=MESH,
        )

    def peer(step):
        return lax.rem(chip + step, 4) * CORES + core

    for g in range(GROUPS):
        push(head, g, peer(1), 1).start()
        push(head, g, peer(3), 3).start()
        push(head, g, sibling, 0).start()

    pick = (iota((BAGS, BAGS * MSG), 1) == iota((BAGS, BAGS * MSG), 0) * MSG + 4 * CAP).astype(f32)
    told = dot(pick.astype(bf16), inbox[...])
    lane_w = iota((BAGS, COUT), 1)
    row_w = iota((BAGS, COUT), 0)
    counts = jnp.where(lane_w < HEAD_DEVS, told, 0.0)
    clip_total = jnp.sum(counts, axis=1, keepdims=True)
    sample = jnp.sum(jnp.where(lane_w == HEAD_DEVS, told, 0.0), axis=1, keepdims=True)
    lower = (iota((COUT, COUT), 0) < iota((COUT, COUT), 1)).astype(f32)
    earlier = dot(counts.astype(bf16), lower.astype(bf16))

    def turned(column_of):
        return jnp.sum(jnp.where(row_w == lane_w, column_of, 0.0), axis=0, keepdims=True)

    sample_row = turned(sample + 1.0) - 1.0
    same_before = (sample_row == sample) & (lane_w < row_w)
    first = jnp.sum(jnp.where(same_before, 1.0 * PER_BAG, 0.0), axis=1, keepdims=True)
    plan_lane = iota((1, COUT), 1)
    start = jnp.zeros((1, 1), f32)
    by_sample = jnp.zeros((1, COUT), f32)
    for s in range(4):
        first = first + jnp.where(sample == s, start, 0.0)
        size = jnp.sum(jnp.where(sample == s, 1.0 * PER_BAG, 0.0), axis=0, keepdims=True)
        by_sample = by_sample + jnp.where(plan_lane == s, start, 0.0)
        by_sample = by_sample + jnp.where(plan_lane == 8 + s, size, 0.0)
        start = start + jnp.ceil(size * (1.0 / ALIGN)) * ALIGN
    plan_row = iota((8, COUT), 0)
    plan = jnp.where(plan_row == 0, turned(first), jnp.where(plan_row == 1, by_sample, 0.0))
    plan_ref[...] = plan.astype(i32)
    key = iota((BAGS, SORTED), 1).astype(f32)
    held = (key >= first) & (key < first + clip_total)
    valid_ref[...] = jnp.sum(held.astype(f32), axis=0, keepdims=True)

    col = iota((8, GROUP), 1)
    col_head = lax.shift_right_logical(col * 1366, 16)
    in_piece = col - col_head * PIECE
    col_clip = lax.shift_right_logical(in_piece * 10923, 16)
    col_slot = (in_piece - col_clip * CAP).astype(f32)
    clip_row = iota((8, GROUP), 0)
    out_at = iota((GROUP, GROUP), 0).astype(f32)
    for g in range(GROUPS):
        group_counts = counts[g * 8 : (g + 1) * 8]
        group_earlier = earlier[g * 8 : (g + 1) * 8]
        number = jnp.zeros((8, GROUP), f32)
        base = jnp.zeros((8, GROUP), f32)
        for h in range(HEAD_DEVS):
            number = jnp.where(col_head == h, group_counts[:, h : h + 1], number)
            base = jnp.where(col_head == h, group_earlier[:, h : h + 1], base)
        place = jnp.where(col_slot < number, clip_row * 1.0 * PER_BAG + base + col_slot + 1.0, 0.0)
        target = jnp.sum(jnp.where(col_clip == clip_row, place, 0.0), axis=0, keepdims=True) - 1.0
        targets[g * 8 : g * 8 + 8] = jnp.broadcast_to(target, (8, GROUP))

    def arrived(of, g):
        pltpu.make_async_copy(piece(of, g), piece(of, g), head_recv.at[g, of]).wait()

    def relay_near(g):
        arrived(peer(1), g)
        arrived(peer(3), g)
        push(peer(3 - 2 * core), g, peer(1 + 2 * core), 2).start()
        push(peer(1), g, sibling, 4).start()
        push(peer(3), g, sibling, 5).start()

    def relay_far(g):
        arrived(peer(2), g)
        push(peer(2), g, sibling, 6).start()

    for load in weights:
        load.wait()
    relay_near(0)
    relay_near(1)
    relay_far(0)

    def stores(g):
        at = pl.ds(pl.multiple_of(g * GROUP, GROUP), GROUP)
        return [
            pltpu.make_async_copy(made.at[at], out.at[at], store_sem.at[m])
            for m, (made, out) in enumerate(((q_ref, q_out), (k_ref, k_out), (v_ref, v_out)))
        ]

    def project(g, carry):
        for step in range(4):
            arrived(lax.rem(chip + step, 4) * CORES + 1 - core, g)
        at = pl.ds(pl.multiple_of(g * GROUP, GROUP), GROUP)
        target = targets[pl.ds(pl.multiple_of(g * 8, 8), 8)][0:1]
        chosen = (out_at == target).astype(f32).astype(bf16)
        cells = dot(chosen, rows[at]).astype(bf16)
        embedded = dot(cells, embed[...]).astype(bf16).astype(f32)

        @pl.when(g < GROUPS - 2)
        def _():
            relay_near(g + 2)

        @pl.when(g < GROUPS - 1)
        def _():
            relay_far(g + 1)

        scale = lax.rsqrt(jnp.mean(embedded * embedded, axis=-1, keepdims=True) + epsilon)
        normed[...] = (embedded * scale).astype(bf16)
        q_ref[at] = (dot(normed[...], qkv[0]).astype(bf16) * HDIM**-0.5).astype(bf16)
        k_ref[at] = dot(normed[...], qkv[1]).astype(bf16)
        v_ref[at] = dot(normed[...], qkv[2]).astype(bf16)
        for store in stores(g):
            store.start()
        return carry

    lax.fori_loop(0, GROUPS, project, 0)

    own_pieces = rows.at[pl.ds(0, GROUPS * PIECE)]
    for sem in range(7):
        pltpu.make_async_copy(own_pieces, own_pieces, head_send.at[sem]).wait()
    for m, (made, out) in enumerate(((q_ref, q_out), (k_ref, k_out), (v_ref, v_out))):
        pltpu.make_async_copy(made, out, store_sem.at[m]).wait()
    sent = outbox.at[pl.ds(0, (BAGS - 1) * MSG)]
    pltpu.make_async_copy(sent, sent, bag_send).wait()

    @pl.when(head < HEAD_DEVS - 1)
    def _():
        to_right.wait_send()

    @pl.when(head > 0)
    def _():
        to_left.wait_send()


def bag_kernel(plan_ref, valid_ref, q_in, k_in, v_in, out_ref, q_ref, k_ref, v_ref, o_ref, load_sem):
    moves = ((k_in, k_ref, 0), (q_in, q_ref, 1), (v_in, v_ref, 2))

    def load(c, carry):
        here = pl.ds(pl.multiple_of(c * PER_BAG, PER_BAG), PER_BAG)
        there = pl.ds(pl.multiple_of(plan_ref[0, c], 16), PER_BAG)
        for source, target, sem in moves:
            pltpu.make_async_copy(source.at[here], target.at[there], load_sem.at[sem]).start()
        return carry

    for s in range(4):
        past = pl.multiple_of(plan_ref[1, s] + plan_ref[1, 8 + s], 16)
        v_ref[pl.ds(past, KTILE)] = jnp.zeros((KTILE, WIDTH), bf16)
    lax.fori_loop(0, BAGS, load, 0)
    for source, target, sem in moves:
        pltpu.make_async_copy(source, target.at[pl.ds(0, SLOTS)], load_sem.at[sem]).wait()

    heads = WIDTH // HDIM
    head_of = lax.shift_right_logical(iota((QTILE, WIDTH), 1), 6)

    def one_sample(s, sample_carry):
        start, size = plan_ref[1, s], plan_ref[1, 8 + s]

        def queries(tile, carry):
            q0 = pl.multiple_of(start + tile * QTILE, ALIGN)
            block = q_ref[pl.ds(q0, QTILE)].astype(f32)
            spread = [jnp.where(head_of == h, block, 0.0).astype(bf16) for h in range(heads)]

            def score(step, h):
                k0 = pl.multiple_of(start + step * KTILE, ALIGN)
                scores = lax.dot_general(
                    spread[h], k_ref[pl.ds(k0, KTILE)], (((1,), (1,)), ((), ())), preferred_element_type=f32
                )
                in_sample = iota((1, KTILE), 1) + step * KTILE < size
                allowed = (valid_ref[:, pl.ds(k0, KTILE)] > 0.0) & in_sample
                scores = jnp.where(allowed, scores, far_below)
                return scores, v_ref[pl.ds(k0, KTILE)]

            steps = lax.div(size + KTILE - 1, KTILE)

            def first(h):
                scores, values = score(0, h)
                top = jnp.max(scores, axis=-1, keepdims=True)
                shifted = jnp.exp(scores - top)
                norm = jnp.sum(shifted, axis=-1, keepdims=True)
                return top, norm, dot(shifted.astype(bf16), values)

            def keys(step, states):
                out = []
                for h in range(heads):
                    top, norm, total = states[h]
                    scores, values = score(step, h)
                    higher = jnp.maximum(top, jnp.max(scores, axis=-1, keepdims=True))
                    shifted = jnp.exp(scores - higher)
                    fade = jnp.exp(top - higher)
                    norm = norm * fade + jnp.sum(shifted, axis=-1, keepdims=True)
                    total = total * fade + dot(shifted.astype(bf16), values)
                    out.append((higher, norm, total))
                return tuple(out)

            def finish(states):
                mixed = jnp.zeros((QTILE, WIDTH), f32)
                for h in range(heads):
                    top, norm, total = states[h]
                    mixed = jnp.where(head_of == h, total * (1.0 / norm), mixed)
                o_ref[pl.ds(q0, QTILE)] = mixed.astype(bf16)

            @pl.when(steps == 1)
            def _():
                mixed = jnp.zeros((QTILE, WIDTH), f32)
                for h in range(heads):
                    top, norm, total = first(h)
                    mixed = jnp.where(head_of == h, total * (1.0 / norm), mixed)
                o_ref[pl.ds(q0, QTILE)] = mixed.astype(bf16)

            @pl.when(steps > 1)
            def _():
                finish(lax.fori_loop(1, steps, keys, tuple(first(h) for h in range(heads))))

            return carry

        lax.fori_loop(0, lax.div(size + QTILE - 1, QTILE), queries, 0)
        return sample_carry

    lax.fori_loop(0, 4, one_sample, 0)

    for c in range(BAGS):
        there = pl.ds(pl.multiple_of(plan_ref[0, c], 16), PER_BAG)
        for half in range(2):
            out_ref[half, c * PER_BAG : (c + 1) * PER_BAG] = o_ref[there, half * COUT : (half + 1) * COUT]


def back_kernel(
    count_ref,
    routes_ref,
    mixed_ref,
    out_ref,
    inbox,
    gather,
    home,
    bag_send,
    bag_recv,
    local_sem,
    head_send,
    head_recv,
):
    bag = lax.axis_index("bag")
    head = lax.axis_index("head")
    count = count_ref[0]
    greet(bag, head)
    met()

    def message(ref, half, at):
        return ref.at[half, pl.ds(pl.multiple_of(at * PER_BAG, PER_BAG), PER_BAG)]

    owns = []
    for half in range(2):

        def send(step, carry, half=half):
            to = lax.rem(bag + step, BAGS)
            pltpu.make_async_remote_copy(
                src_ref=message(mixed_ref, half, to),
                dst_ref=message(inbox, half, bag),
                send_sem=bag_send.at[half],
                recv_sem=bag_recv.at[half],
                device_id=(to, head),
                device_id_type=MESH,
            ).start()
            return carry

        lax.fori_loop(1, BAGS, send, 0)
        own = pltpu.make_async_copy(message(mixed_ref, half, bag), message(inbox, half, bag), local_sem.at[half])
        own.start()
        owns.append(own)

    routes_col = jnp.transpose(routes_ref[...])
    half = (iota((TOK, 1), 0) >= TOK // 2).astype(i32)
    before = (iota((TOK, TOK), 1) < iota((TOK, TOK), 0)).astype(bf16)
    at_col = iota((TOK, SLOTS), 1)
    earlier = jnp.zeros((1, TOK), f32)
    for h in range(HEAD_DEVS):
        route = routes_col[:, h : h + 1]
        live = h * FRAMES_DEV + half < count
        named = ((route == iota((TOK, TOK), 1)) & live).astype(f32)
        rank = jnp.sum(named * (dot(before, named.astype(bf16)) + earlier), axis=1, keepdims=True)
        earlier = earlier + jnp.sum(named, axis=0, keepdims=True)
        target = jnp.where(live, route * PER_BAG + rank.astype(i32), -1)
        gather[h * TOK : (h + 1) * TOK] = (at_col == target).astype(f32).astype(bf16)

    def rest(ref, half):
        return ref.at[half, pl.ds(0, (BAGS - 1) * PER_BAG)]

    def columns(half):
        return pl.ds(pl.multiple_of(head * WIDTH + half * COUT, COUT), COUT)

    keeps = []
    for half in range(2):
        owns[half].wait()
        pltpu.make_async_copy(rest(inbox, half), rest(inbox, half), bag_recv.at[half]).wait()

        def deliver(step, carry, half=half):
            to = lax.rem(head + step, HEAD_DEVS)
            at = pl.ds(pl.multiple_of(to * TOK, TOK), TOK)
            home[half, at] = dot(gather[at], inbox[half]).astype(bf16)
            pltpu.make_async_remote_copy(
                src_ref=home.at[half, at],
                dst_ref=out_ref.at[:, columns(half)],
                send_sem=head_send.at[half],
                recv_sem=head_recv.at[half],
                device_id=(bag, to),
                device_id_type=MESH,
            ).start()
            return carry

        lax.fori_loop(1, HEAD_DEVS, deliver, 0)
        at = pl.ds(pl.multiple_of(head * TOK, TOK), TOK)
        home[half, at] = dot(gather[at], inbox[half]).astype(bf16)
        keep = pltpu.make_async_copy(home.at[half, at], out_ref.at[:, columns(half)], local_sem.at[2 + half])
        keep.start()
        keeps.append(keep)
    for half in range(2):
        keeps[half].wait()
        arrived = out_ref.at[:, pl.ds(0, (HEAD_DEVS - 1) * COUT)]
        pltpu.make_async_copy(arrived, arrived, head_recv.at[half]).wait()
        left = home.at[half, pl.ds(0, (HEAD_DEVS - 1) * TOK)]
        pltpu.make_async_copy(left, left, head_send.at[half]).wait()
        pltpu.make_async_copy(rest(mixed_ref, half), rest(mixed_ref, half), bag_send.at[half]).wait()


SMEM = pl.BlockSpec(memory_space=pltpu.SMEM)
VMEM = pl.BlockSpec(memory_space=pltpu.VMEM)
ANY = pl.BlockSpec(memory_space=pl.ANY)


def shards(latents, frame_counts, routes, samples, conv_weight, embed_weight, qkv_weight):
    routes = routes.reshape(HEAD_DEVS, TOK)
    samples = samples.reshape(HEAD_DEVS, TOK)
    latents = latents.reshape(FRAMES_DEV, CELLS, CIN)
    dma = pltpu.SemaphoreType.DMA
    slot_array = jax.ShapeDtypeStruct((SLOTS, WIDTH), bf16)
    q, k, v, plan, valid = pl.pallas_call(
        front_kernel,
        out_shape=(
            slot_array,
            slot_array,
            slot_array,
            jax.ShapeDtypeStruct((8, COUT), i32),
            jax.ShapeDtypeStruct((1, SORTED), f32),
        ),
        in_specs=[SMEM, VMEM, VMEM, ANY, ANY, ANY, ANY],
        out_specs=(ANY, ANY, ANY, VMEM, VMEM),
        scratch_shapes=[
            pltpu.VMEM((3, CIN, 9 * COUT), bf16),
            pltpu.VMEM((FRAMES_DEV, CELLS, CIN), bf16),
            pltpu.VMEM((FRAMES_DEV + 2, 3, CELLS, COUT), f32),
            pltpu.VMEM((2, CELLS, COUT), bf16),
            pltpu.VMEM((2, CELLS, COUT), bf16),
            pltpu.VMEM((FRAMES_DEV * 16, 16, COUT), f32),
            pltpu.VMEM((BAGS * MSG, 4 * TOK), bf16),
            pltpu.VMEM((BAGS * MSG, COUT), bf16),
            pltpu.VMEM((BAGS * MSG, COUT), bf16),
            pltpu.VMEM((4 * ROWS, BAGS * MSG), bf16),
            pltpu.VMEM((SLOTS, CIN), bf16),
            pltpu.VMEM((CIN, D), bf16),
            pltpu.VMEM((3, D, WIDTH), bf16),
            pltpu.VMEM((GROUP, D), bf16),
            pltpu.VMEM((GROUPS * 8, GROUP), f32),
            pltpu.VMEM((SLOTS, WIDTH), bf16),
            pltpu.VMEM((SLOTS, WIDTH), bf16),
            pltpu.VMEM((SLOTS, WIDTH), bf16),
            dma((4,)),
            dma((3,)),
            dma((2,)),
            dma((2,)),
            dma,
            dma,
            dma((1,)),
            dma((7,)),
            dma((GROUPS, HEAD_DEVS)),
            dma((3,)),
        ],
        compiler_params=pltpu.CompilerParams(
            collective_id=0, has_side_effects=True, vmem_limit_bytes=56 << 20
        ),
        name="front",
    )(frame_counts, routes, samples, latents, conv_weight, embed_weight, qkv_weight)
    mixed = pl.pallas_call(
        bag_kernel,
        out_shape=jax.ShapeDtypeStruct((2, SLOTS, COUT), bf16),
        in_specs=[SMEM, VMEM, ANY, ANY, ANY],
        out_specs=VMEM,
        scratch_shapes=[
            pltpu.VMEM((SORTED, WIDTH), bf16),
            pltpu.VMEM((SORTED, WIDTH), bf16),
            pltpu.VMEM((SORTED, WIDTH), bf16),
            pltpu.VMEM((SORTED, WIDTH), bf16),
            dma((3,)),
        ],
        compiler_params=pltpu.CompilerParams(vmem_limit_bytes=56 << 20),
        name="bag",
    )(plan, valid, q, k, v)
    return pl.pallas_call(
        back_kernel,
        out_shape=jax.ShapeDtypeStruct((TOK, D), bf16),
        in_specs=[SMEM, VMEM, ANY],
        out_specs=ANY,
        scratch_shapes=[
            pltpu.VMEM((2, SLOTS, COUT), bf16),
            pltpu.VMEM((HEAD_DEVS * TOK, SLOTS), bf16),
            pltpu.VMEM((2, HEAD_DEVS * TOK, COUT), bf16),
            dma((2,)),
            dma((2,)),
            dma((4,)),
            dma((2,)),
            dma((2,)),
        ],
        compiler_params=pltpu.CompilerParams(
            collective_id=1, has_side_effects=True, vmem_limit_bytes=56 << 20
        ),
        name="back",
    )(frame_counts, routes, mixed)


def solution(mesh):
    placed = (
        P("bag", "head", None, None, None),
        P("bag"),
        P("bag", None),
        P("bag"),
        P(),
        P(),
        P(None, None, "head"),
    )
    return jax.shard_map(
        shards, mesh=mesh, in_specs=placed, out_specs=P(("bag", "head"), None), check_vma=False
    )
```

profile of v0, /device:TPU:1, one launch (start us, length us, event | category | flops | bytes accessed | tf_op | source)
XLA Modules:
  0.0 92.1 jit_solution(16634572037684015947)
XLA Ops:
  0.7 49.0 %front.1 = (bf16[1536,256]{1,0:T(8,128)(2,1)}, bf16[1536,256]{1,0:T(8,128)(2,1)}, bf16[1536,256]{1,0:T(8,128)(2,1)}, s32[8,128]{1,0:T(8,128)}, f32[1,2432]{1,0:T(1,128)}) custom-call(s32[1]{0:T(128)S(6)} %copy.9.count_ref, s32[8,128]{1,0:T(8,128)} %bitcast.4, s32[8,128]{1,0:T(8,128)} %bitcast.6, bf16[2,256,512]{2,1,0:T(8,128)(2,1)} %bitcast.3, ...), custom_call_target="tpu_custom_call" | custom-call | tf_op jit(solution)/shard_map/front/pallas_call | solution.py:623
  49.6 9.3 %bag.1.mixed_ref = bf16[2,1536,128]{2,1,0:T(8,128)(2,1)} custom-call(s32[8,128]{1,0:T(8,128)} %get-tuple-element.10.plan_ref, f32[1,2432]{1,0:T(1,128)} %get-tuple-element.11.valid_ref, bf16[1536,256]{1,0:T(8,128)(2,1)} %get-tuple-element.12.q_in, bf16[1536,256]{1,0:T(8,128)(2,1)} %get-tuple-element.13.k_in, bf16[1536,256]{1,0:T(8,128)(2,1)} %get-tuple-element.14.v_in), custom_call_target="tpu_custom_call" | custom-call | tf_op jit(solution)/shard_map/bag/pallas_call | solution.py:669
  59.0 31.3 %back.1 = bf16[128,2048]{1,0:T(8,128)(2,1)} custom-call(s32[1]{0:T(128)S(6)} %copy.9.count_ref, s32[8,128]{1,0:T(8,128)} %bitcast.5, bf16[2,1536,128]{2,1,0:T(8,128)(2,1)} %bag.1.mixed_ref), custom_call_target="tpu_custom_call" | custom-call | tf_op jit(solution)/shard_map/back/pallas_call | solution.py:684
  90.3 1.9 %copy.10 = bf16[128,2048]{1,0:T(8,128)(2,1)} copy(bf16[128,2048]{1,0:T(8,128)(2,1)} %back.1) | data formatting | bytes 1048576
where the time goes:
time: 92.5 us; the launch traced here: 92.1 us
  Pallas kernels  89.6 us (97%)
  local copies, waits for them, and re-layouts  1.88 us (2%)
    pallas_call x1, Pallas kernels, shards(): pl.pallas_call(front_kernel, out_shape=(slot_array, slot_array, slot_arra...  49 us
    pallas_call x1, Pallas kernels, shards(): pl.pallas_call(back_kernel, out_shape=jax.ShapeDtypeStruct((TOK, D), bf16...  31.3 us
    pallas_call x1, Pallas kernels, shards(): pl.pallas_call(bag_kernel, out_shape=jax.ShapeDtypeStruct((2, SLOTS, COUT...  9.3 us
    unnamed x1, local copies, waits for them, and re-layouts  1.88 us

commit v1 on v0

--- a/solution.py
+++ b/solution.py
@@ -97,9 +97,8 @@
     qkv,
     normed,
     targets,
-    q_ref,
-    k_ref,
-    v_ref,
+    raw,
+    sorted_rows,
     load_sem,
     tap_sem,
     halo_send,
@@ -162,11 +161,11 @@
     loads[0].wait()
     taps_here(2)
     add_taps(0, 2, 2)
-    edge_out[1] = joined(2).astype(bf16)
+    edge_out[1] = joined(2)
     loads[1].wait()
     taps_here(0)
     add_taps(1, 0, 3)
-    edge_out[0] = joined(3).astype(bf16)
+    edge_out[0] = joined(3)
     met()
 
     def edge(side, to):
@@ -225,7 +224,7 @@
 
     for f in range(FRAMES_DEV):
         scale = jnp.where(head * FRAMES_DEV + f < count, 1.0, 0.0)
-        total = (joined(f) + edge_in[f].astype(f32)) * scale
+        total = (joined(f) + edge_in[f]) * scale
         grid[f * 16 : (f + 1) * 16] = total.reshape(16, 16, COUT)
     quarters = []
     for di in range(2):
@@ -267,24 +266,22 @@
     others = inbox.at[pl.ds(0, (BAGS - 1) * MSG)]
     pltpu.make_async_copy(others, others, bag_recv).wait()
 
-    def piece(of, group):
-        return rows.at[pl.ds(pl.multiple_of(group * GROUP + of * PIECE, PIECE), PIECE)]
+    def chunk(of):
+        return rows.at[pl.ds(pl.multiple_of(of * ROWS, ROWS), ROWS)]
 
     unpacked = dot(unpack[...], inbox[...]).astype(bf16)
-    for g in range(GROUPS):
-        at = pl.ds(pl.multiple_of(g * GROUP + head * PIECE, PIECE), PIECE)
-        for q in range(4):
-            first_row = q * ROWS + g * PIECE
-            rows[at, q * COUT : (q + 1) * COUT] = unpacked[first_row : first_row + PIECE]
+    at = pl.ds(pl.multiple_of(head * ROWS, ROWS), ROWS)
+    for q in range(4):
+        rows[at, q * COUT : (q + 1) * COUT] = unpacked[q * ROWS : (q + 1) * ROWS]
 
     sibling = chip * CORES + 1 - core
 
-    def push(of, group, to, sem):
+    def push(of, to, sem):
         return pltpu.make_async_remote_copy(
-            src_ref=piece(of, group),
-            dst_ref=piece(of, group),
+            src_ref=chunk(of),
+            dst_ref=chunk(of),
             send_sem=head_send.at[sem],
-            recv_sem=head_recv.at[group, of],
+            recv_sem=head_recv.at[of],
             device_id=(bag, to),
             device_id_type=MESH,
         )
@@ -292,10 +289,9 @@
     def peer(step):
         return lax.rem(chip + step, 4) * CORES + core
 
-    for g in range(GROUPS):
-        push(head, g, peer(1), 1).start()
-        push(head, g, peer(3), 3).start()
-        push(head, g, sibling, 0).start()
+    push(head, sibling, 0).start()
+    push(head, peer(1), 1).start()
+    push(head, peer(3), 3).start()
 
     pick = (iota((BAGS, BAGS * MSG), 1) == iota((BAGS, BAGS * MSG), 0) * MSG + 4 * CAP).astype(f32)
     told = dot(pick.astype(bf16), inbox[...])
@@ -348,66 +344,70 @@
         target = jnp.sum(jnp.where(col_clip == clip_row, place, 0.0), axis=0, keepdims=True) - 1.0
         targets[g * 8 : g * 8 + 8] = jnp.broadcast_to(target, (8, GROUP))
 
-    def arrived(of, g):
-        pltpu.make_async_copy(piece(of, g), piece(of, g), head_recv.at[g, of]).wait()
-
-    def relay_near(g):
-        arrived(peer(1), g)
-        arrived(peer(3), g)
-        push(peer(3 - 2 * core), g, peer(1 + 2 * core), 2).start()
-        push(peer(1), g, sibling, 4).start()
-        push(peer(3), g, sibling, 5).start()
-
-    def relay_far(g):
-        arrived(peer(2), g)
-        push(peer(2), g, sibling, 6).start()
+    def arrived(of):
+        pltpu.make_async_copy(chunk(of), chunk(of), head_recv.at[of]).wait()
+
+    def relay_near():
+        arrived(peer(1))
+        arrived(peer(3))
+        push(peer(1), sibling, 4).start()
+        push(peer(3), sibling, 5).start()
+        push(peer(3 - 2 * core), peer(1 + 2 * core), 2).start()
+
+    def relay_far():
+        arrived(peer(2))
+        push(peer(2), sibling, 6).start()
 
     for load in weights:
         load.wait()
-    relay_near(0)
-    relay_near(1)
-    relay_far(0)
-
-    def stores(g):
-        at = pl.ds(pl.multiple_of(g * GROUP, GROUP), GROUP)
-        return [
-            pltpu.make_async_copy(made.at[at], out.at[at], store_sem.at[m])
-            for m, (made, out) in enumerate(((q_ref, q_out), (k_ref, k_out), (v_ref, v_out)))
-        ]
-
-    def project(g, carry):
-        for step in range(4):
-            arrived(lax.rem(chip + step, 4) * CORES + 1 - core, g)
+
+    def project(k, carry):
+        of_chip = lax.rem(chip + k + k // 2 * (5 - 2 * k), 4)
+        arrived(of_chip * CORES + 1 - core)
+        for c in range(CORES):
+            of = pl.ds(pl.multiple_of((of_chip * CORES + c) * ROWS, ROWS), ROWS)
+            embedded = dot(rows[of], embed[...]).astype(bf16).astype(f32)
+            scale = lax.rsqrt(jnp.mean(embedded * embedded, axis=-1, keepdims=True) + epsilon)
+            normed[c * ROWS : (c + 1) * ROWS] = (embedded * scale).astype(bf16)
+        for c in range(CORES):
+            for m in range(3):
+                made = dot(normed[c * ROWS : (c + 1) * ROWS], qkv[m]).astype(bf16)
+                if m == 0:
+                    made = (made * HDIM**-0.5).astype(bf16)
+                for g in range(GROUPS):
+                    at = g * GROUP + (of_chip * CORES + c) * PIECE
+                    part = made[g * PIECE : (g + 1) * PIECE]
+                    raw[pl.ds(pl.multiple_of(at, PIECE), PIECE), m * WIDTH : (m + 1) * WIDTH] = part
+
+        @pl.when(k == 0)
+        def _():
+            relay_near()
+
+        @pl.when(k == 1)
+        def _():
+            relay_far()
+
+        return carry
+
+    lax.fori_loop(0, GROUPS, project, 0)
+
+    outs = (q_out, k_out, v_out)
+
+    def order(g, carry):
         at = pl.ds(pl.multiple_of(g * GROUP, GROUP), GROUP)
         target = targets[pl.ds(pl.multiple_of(g * 8, 8), 8)][0:1]
         chosen = (out_at == target).astype(f32).astype(bf16)
-        cells = dot(chosen, rows[at]).astype(bf16)
-        embedded = dot(cells, embed[...]).astype(bf16).astype(f32)
-
-        @pl.when(g < GROUPS - 2)
-        def _():
-            relay_near(g + 2)
-
-        @pl.when(g < GROUPS - 1)
-        def _():
-            relay_far(g + 1)
-
-        scale = lax.rsqrt(jnp.mean(embedded * embedded, axis=-1, keepdims=True) + epsilon)
-        normed[...] = (embedded * scale).astype(bf16)
-        q_ref[at] = (dot(normed[...], qkv[0]).astype(bf16) * HDIM**-0.5).astype(bf16)
-        k_ref[at] = dot(normed[...], qkv[1]).astype(bf16)
-        v_ref[at] = dot(normed[...], qkv[2]).astype(bf16)
-        for store in stores(g):
-            store.start()
+        for m in range(3):
+            sorted_rows[m, at] = dot(chosen, raw[at, m * WIDTH : (m + 1) * WIDTH]).astype(bf16)
+            pltpu.make_async_copy(sorted_rows.at[m, at], outs[m].at[at], store_sem.at[m]).start()
         return carry
 
-    lax.fori_loop(0, GROUPS, project, 0)
-
-    own_pieces = rows.at[pl.ds(0, GROUPS * PIECE)]
+    lax.fori_loop(0, GROUPS, order, 0)
+
     for sem in range(7):
-        pltpu.make_async_copy(own_pieces, own_pieces, head_send.at[sem]).wait()
-    for m, (made, out) in enumerate(((q_ref, q_out), (k_ref, k_out), (v_ref, v_out))):
-        pltpu.make_async_copy(made, out, store_sem.at[m]).wait()
+        pltpu.make_async_copy(chunk(0), chunk(0), head_send.at[sem]).wait()
+    for m in range(3):
+        pltpu.make_async_copy(sorted_rows.at[m], outs[m], store_sem.at[m]).wait()
     sent = outbox.at[pl.ds(0, (BAGS - 1) * MSG)]
     pltpu.make_async_copy(sent, sent, bag_send).wait()
 
@@ -635,8 +635,8 @@
             pltpu.VMEM((3, CIN, 9 * COUT), bf16),
             pltpu.VMEM((FRAMES_DEV, CELLS, CIN), bf16),
             pltpu.VMEM((FRAMES_DEV + 2, 3, CELLS, COUT), f32),
-            pltpu.VMEM((2, CELLS, COUT), bf16),
-            pltpu.VMEM((2, CELLS, COUT), bf16),
+            pltpu.VMEM((2, CELLS, COUT), f32),
+            pltpu.VMEM((2, CELLS, COUT), f32),
             pltpu.VMEM((FRAMES_DEV * 16, 16, COUT), f32),
             pltpu.VMEM((BAGS * MSG, 4 * TOK), bf16),
             pltpu.VMEM((BAGS * MSG, COUT), bf16),
@@ -647,9 +647,8 @@
             pltpu.VMEM((3, D, WIDTH), bf16),
             pltpu.VMEM((GROUP, D), bf16),
             pltpu.VMEM((GROUPS * 8, GROUP), f32),
-            pltpu.VMEM((SLOTS, WIDTH), bf16),
-            pltpu.VMEM((SLOTS, WIDTH), bf16),
-            pltpu.VMEM((SLOTS, WIDTH), bf16),
+            pltpu.VMEM((SLOTS, 3 * WIDTH), bf16),
+            pltpu.VMEM((3, SLOTS, WIDTH), bf16),
             dma((4,)),
             dma((3,)),
             dma((2,)),
@@ -658,7 +657,7 @@
             dma,
             dma((1,)),
             dma((7,)),
-            dma((GROUPS, HEAD_DEVS)),
+            dma((HEAD_DEVS,)),
             dma((3,)),
         ],
         compiler_params=pltpu.CompilerParams(

time: 92.5 us -> 86.7 us (0.937)
  Pallas kernels: 89.6 us -> 83.8 us
    pallas_call x1, Pallas kernels: 49 us -> 43.5 us  [shards(): pl.pallas_call(front_kernel, out_shape=(slot_array, slot_array, slot_arra...]
where the time goes in v1:
time: 86.7 us; the launch traced here: 86.3 us
  Pallas kernels  83.8 us (97%)
  local copies, waits for them, and re-layouts  1.88 us (2%)
    pallas_call x1, Pallas kernels, shards(): pl.pallas_call(front_kernel, out_shape=(slot_array, slot_array, slot_arra...  43.5 us
    pallas_call x1, Pallas kernels, shards(): pl.pallas_call(back_kernel, out_shape=jax.ShapeDtypeStruct((TOK, D), bf16...  31 us
    pallas_call x1, Pallas kernels, shards(): pl.pallas_call(bag_kernel, out_shape=jax.ShapeDtypeStruct((2, SLOTS, COUT...  9.29 us
    unnamed x1, local copies, waits for them, and re-layouts  1.88 us

profile of v1, /device:TPU:1, one launch (start us, length us, event | category | flops | bytes accessed | tf_op | source)
XLA Modules:
  0.0 86.3 jit_solution(15401067801861150570)
XLA Ops:
  0.7 43.5 %front.1 = (bf16[1536,256]{1,0:T(8,128)(2,1)}, bf16[1536,256]{1,0:T(8,128)(2,1)}, bf16[1536,256]{1,0:T(8,128)(2,1)}, s32[8,128]{1,0:T(8,128)}, f32[1,2432]{1,0:T(1,128)}) custom-call(s32[1]{0:T(128)S(6)} %copy.9.count_ref, s32[8,128]{1,0:T(8,128)} %bitcast.4, s32[8,128]{1,0:T(8,128)} %bitcast.6, bf16[2,256,512]{2,1,0:T(8,128)(2,1)} %bitcast.3, ...), custom_call_target="tpu_custom_call" | custom-call | tf_op jit(solution)/shard_map/front/pallas_call | solution.py:623
  44.1 9.3 %bag.1.mixed_ref = bf16[2,1536,128]{2,1,0:T(8,128)(2,1)} custom-call(s32[8,128]{1,0:T(8,128)} %get-tuple-element.10.plan_ref, f32[1,2432]{1,0:T(1,128)} %get-tuple-element.11.valid_ref, bf16[1536,256]{1,0:T(8,128)(2,1)} %get-tuple-element.12.q_in, bf16[1536,256]{1,0:T(8,128)(2,1)} %get-tuple-element.13.k_in, bf16[1536,256]{1,0:T(8,128)(2,1)} %get-tuple-element.14.v_in), custom_call_target="tpu_custom_call" | custom-call | tf_op jit(solution)/shard_map/bag/pallas_call | solution.py:668
  53.4 31.0 %back.1 = bf16[128,2048]{1,0:T(8,128)(2,1)} custom-call(s32[1]{0:T(128)S(6)} %copy.9.count_ref, s32[8,128]{1,0:T(8,128)} %bitcast.5, bf16[2,1536,128]{2,1,0:T(8,128)(2,1)} %bag.1.mixed_ref), custom_call_target="tpu_custom_call" | custom-call | tf_op jit(solution)/shard_map/back/pallas_call | solution.py:683
  84.4 1.9 %copy.10 = bf16[128,2048]{1,0:T(8,128)(2,1)} copy(bf16[128,2048]{1,0:T(8,128)(2,1)} %back.1) | data formatting | bytes 1048576

commit v2 on v1

--- a/solution.py
+++ b/solution.py
@@ -132,9 +132,6 @@
         pltpu.make_async_copy(embed_ref, embed, load_sem.at[2]),
         pltpu.make_async_copy(qkv_ref, qkv, load_sem.at[3]),
     ]
-    for load in weights:
-        load.start()
-
     edge_in[...] = jnp.zeros_like(edge_in)
     greet(bag, head)
 
@@ -156,38 +153,6 @@
         from_left = jnp.where(column == 0, 0.0, pltpu.roll(sums[out, 0], 1, 0))
         from_right = jnp.where(column == 15, 0.0, pltpu.roll(sums[out, 2], CELLS - 1, 0))
         return sums[out, 1] + from_left + from_right
-
-    sums[...] = jnp.zeros_like(sums)
-    loads[0].wait()
-    taps_here(2)
-    add_taps(0, 2, 2)
-    edge_out[1] = joined(2)
-    loads[1].wait()
-    taps_here(0)
-    add_taps(1, 0, 3)
-    edge_out[0] = joined(3)
-    met()
-
-    def edge(side, to):
-        return pltpu.make_async_remote_copy(
-            src_ref=edge_out.at[side],
-            dst_ref=edge_in.at[side],
-            send_sem=halo_send.at[side],
-            recv_sem=halo_recv.at[side],
-            device_id=(bag, to),
-            device_id_type=MESH,
-        )
-
-    to_right = edge(0, lax.rem(head + 1, HEAD_DEVS))
-    to_left = edge(1, lax.rem(head + HEAD_DEVS - 1, HEAD_DEVS))
-
-    @pl.when(head < HEAD_DEVS - 1)
-    def _():
-        to_right.start()
-
-    @pl.when(head > 0)
-    def _():
-        to_left.start()
 
     lane = iota((1, TOK), 1)
     bag_row = iota((BAGS, TOK), 0)
@@ -208,9 +173,43 @@
     for q in range(4):
         scatter[:, q * TOK : (q + 1) * TOK] = (out_row == target + CAP * q).astype(f32).astype(bf16)
 
+    sums[...] = jnp.zeros_like(sums)
+    loads[0].wait()
+    taps_here(2)
+    add_taps(0, 2, 2)
+    edge_out[1] = joined(2)
+    loads[1].wait()
+    taps_here(0)
+    add_taps(1, 0, 3)
+    edge_out[0] = joined(3)
+    met()
+
+    def edge(side, to):
+        return pltpu.make_async_remote_copy(
+            src_ref=edge_out.at[side],
+            dst_ref=edge_in.at[side],
+            send_sem=halo_send.at[side],
+            recv_sem=halo_recv.at[side],
+            device_id=(bag, to),
+            device_id_type=MESH,
+        )
+
+    to_right = edge(0, lax.rem(head + 1, HEAD_DEVS))
+    to_left = edge(1, lax.rem(head + HEAD_DEVS - 1, HEAD_DEVS))
+
+    @pl.when(head < HEAD_DEVS - 1)
+    def _():
+        to_right.start()
+
+    @pl.when(head > 0)
+    def _():
+        to_left.start()
+
     add_taps(0, 0, 1)
     add_taps(1, 2, 0)
     taps_here(1)
+    for load in weights:
+        load.start()
     add_taps(0, 1, 0)
     add_taps(1, 1, 1)
 
@@ -667,7 +666,7 @@
     )(frame_counts, routes, samples, latents, conv_weight, embed_weight, qkv_weight)
     mixed = pl.pallas_call(
         bag_kernel,
-        out_shape=jax.ShapeDtypeStruct((2, SLOTS, COUT), bf16),
+        out_shape=pltpu.VMEM((2, SLOTS, COUT), bf16),
         in_specs=[SMEM, VMEM, ANY, ANY, ANY],
         out_specs=VMEM,
         scratch_shapes=[
@@ -682,7 +681,7 @@
     )(plan, valid, q, k, v)
     return pl.pallas_call(
         back_kernel,
-        out_shape=jax.ShapeDtypeStruct((TOK, D), bf16),
+        out_shape=pltpu.VMEM((TOK, D), bf16),
         in_specs=[SMEM, VMEM, ANY],
         out_specs=ANY,
         scratch_shapes=[
@@ -696,7 +695,7 @@
             dma((2,)),
         ],
         compiler_params=pltpu.CompilerParams(
-            collective_id=1, has_side_effects=True, vmem_limit_bytes=56 << 20
+            collective_id=1, has_side_effects=True, vmem_limit_bytes=40 << 20
         ),
         name="back",
     )(frame_counts, routes, mixed)

time: 86.7 us -> 84 us (0.969)
  Pallas kernels: 83.8 us -> 82.2 us
  local copies, waits for them, and re-layouts: 1.88 us -> 0.8 us
    pallas_call x2, Pallas kernels: 40.3 us -> 38.7 us  [the longest x1 30.2 us: shards(): pl.pallas_call(back_kernel, out_shape=pltpu.VMEM((TOK, D), bf16), in_spec...]
    unnamed x1 -> x3, local copies, waits for them, and re-layouts: 1.88 us -> 0.8 us
where the time goes in v2:
time: 84 us; the launch traced here: 83.7 us
  Pallas kernels  82.2 us (98%)
    pallas_call x1, Pallas kernels, shards(): pl.pallas_call(front_kernel, out_shape=(slot_array, slot_array, slot_arra...  43.5 us
    pallas_call x1, Pallas kernels, shards(): pl.pallas_call(back_kernel, out_shape=pltpu.VMEM((TOK, D), bf16), in_spec...  30.2 us
    pallas_call x1, Pallas kernels, shards(): pl.pallas_call(bag_kernel, out_shape=pltpu.VMEM((2, SLOTS, COUT), bf16),...  8.55 us

profile of v2, /device:TPU:1, one launch (start us, length us, event | category | flops | bytes accessed | tf_op | source)
XLA Modules:
  0.0 83.7 jit_solution(6427693699695760613)
XLA Ops:
  0.7 43.5 %front.1 = (bf16[1536,256]{1,0:T(8,128)(2,1)}, bf16[1536,256]{1,0:T(8,128)(2,1)}, bf16[1536,256]{1,0:T(8,128)(2,1)}, s32[8,128]{1,0:T(8,128)}, f32[1,2432]{1,0:T(1,128)}) custom-call(s32[1]{0:T(128)S(6)} %copy.10.count_ref, s32[8,128]{1,0:T(8,128)} %bitcast.3, s32[8,128]{1,0:T(8,128)} %bitcast.6, bf16[2,256,512]{2,1,0:T(8,128)(2,1)} %bitcast.5, ...), custom_call_target="tpu_custom_call" | custom-call | tf_op jit(solution)/shard_map/front/pallas_call | solution.py:622
  44.1 0.0 copy-start
  44.1 8.5 %bag.1.mixed_ref = bf16[2,1536,128]{2,1,0:T(8,128)(2,1)S(1)} custom-call(s32[8,128]{1,0:T(8,128)} %get-tuple-element.10.plan_ref, f32[1,2432]{1,0:T(1,128)} %get-tuple-element.11.valid_ref, bf16[1536,256]{1,0:T(8,128)(2,1)} %get-tuple-element.12.q_in, bf16[1536,256]{1,0:T(8,128)(2,1)} %get-tuple-element.13.k_in, bf16[1536,256]{1,0:T(8,128)(2,1)} %get-tuple-element.14.v_in), custom_call_target="tpu_custom_call" | custom-call | tf_op jit(solution)/shard_map/bag/pallas_call | solution.py:667
  52.7 0.0 copy-done
  52.7 30.2 %back.1 = bf16[128,2048]{1,0:T(8,128)(2,1)S(1)} custom-call(s32[1]{0:T(128)S(6)} %copy.10.count_ref, s32[8,128]{1,0:T(8,128)S(1)} %bitcast.4, bf16[2,1536,128]{2,1,0:T(8,128)(2,1)S(1)} %bag.1.mixed_ref), custom_call_target="tpu_custom_call" | custom-call | tf_op jit(solution)/shard_map/back/pallas_call | solution.py:682
  82.9 0.8 copy.9
Async XLA Ops:
  44.1 8.6 %copy-start = (s32[1024,1]{0,1:T(1,128)S(1)}, s32[1024,1]{0,1:T(1,128)}, u32[]{:S(2)}) copy-start(s32[1024,1]{0,1:T(1,128)} %param.9) | copy-start | bytes 12292

commit v3 on v2

--- a/solution.py
+++ b/solution.py
@@ -341,7 +341,7 @@
             base = jnp.where(col_head == h, group_earlier[:, h : h + 1], base)
         place = jnp.where(col_slot < number, clip_row * 1.0 * PER_BAG + base + col_slot + 1.0, 0.0)
         target = jnp.sum(jnp.where(col_clip == clip_row, place, 0.0), axis=0, keepdims=True) - 1.0
-        targets[g * 8 : g * 8 + 8] = jnp.broadcast_to(target, (8, GROUP))
+        targets[g * GROUP : (g + 1) * GROUP] = (out_at == target).astype(f32).astype(bf16)
 
     def arrived(of):
         pltpu.make_async_copy(chunk(of), chunk(of), head_recv.at[of]).wait()
@@ -394,14 +394,14 @@
 
     def order(g, carry):
         at = pl.ds(pl.multiple_of(g * GROUP, GROUP), GROUP)
-        target = targets[pl.ds(pl.multiple_of(g * 8, 8), 8)][0:1]
-        chosen = (out_at == target).astype(f32).astype(bf16)
+        chosen = targets[at]
         for m in range(3):
             sorted_rows[m, at] = dot(chosen, raw[at, m * WIDTH : (m + 1) * WIDTH]).astype(bf16)
             pltpu.make_async_copy(sorted_rows.at[m, at], outs[m].at[at], store_sem.at[m]).start()
         return carry
 
-    lax.fori_loop(0, GROUPS, order, 0)
+    for g in range(GROUPS):
+        order(g, 0)
 
     for sem in range(7):
         pltpu.make_async_copy(chunk(0), chunk(0), head_send.at[sem]).wait()
@@ -645,7 +645,7 @@
             pltpu.VMEM((CIN, D), bf16),
             pltpu.VMEM((3, D, WIDTH), bf16),
             pltpu.VMEM((GROUP, D), bf16),
-            pltpu.VMEM((GROUPS * 8, GROUP), f32),
+            pltpu.VMEM((GROUPS * GROUP, GROUP), bf16),
             pltpu.VMEM((SLOTS, 3 * WIDTH), bf16),
             pltpu.VMEM((3, SLOTS, WIDTH), bf16),
             dma((4,)),

time: 84 us -> 83.5 us (level)
  no operation moved by 1% of the time
where the time goes in v3:
time: 83.5 us; the launch traced here: 83.2 us
  Pallas kernels  81.7 us (98%)
    pallas_call x1, Pallas kernels, shards(): pl.pallas_call(front_kernel, out_shape=(slot_array, slot_array, slot_arra...  43 us
    pallas_call x1, Pallas kernels, shards(): pl.pallas_call(back_kernel, out_shape=pltpu.VMEM((TOK, D), bf16), in_spec...  30.2 us
    pallas_call x1, Pallas kernels, shards(): pl.pallas_call(bag_kernel, out_shape=pltpu.VMEM((2, SLOTS, COUT), bf16),...  8.55 us

profile of v3, /device:TPU:1, one launch (start us, length us, event | category | flops | bytes accessed | tf_op | source)
XLA Modules:
  0.0 83.2 jit_solution(15018808247126134171)
XLA Ops:
  0.7 43.0 %front.1 = (bf16[1536,256]{1,0:T(8,128)(2,1)}, bf16[1536,256]{1,0:T(8,128)(2,1)}, bf16[1536,256]{1,0:T(8,128)(2,1)}, s32[8,128]{1,0:T(8,128)}, f32[1,2432]{1,0:T(1,128)}) custom-call(s32[1]{0:T(128)S(6)} %copy.10.count_ref, s32[8,128]{1,0:T(8,128)} %bitcast.3, s32[8,128]{1,0:T(8,128)} %bitcast.6, bf16[2,256,512]{2,1,0:T(8,128)(2,1)} %bitcast.5, ...), custom_call_target="tpu_custom_call" | custom-call | tf_op jit(solution)/shard_map/front/pallas_call | solution.py:622
  43.7 0.0 copy-start
  43.7 8.5 %bag.1.mixed_ref = bf16[2,1536,128]{2,1,0:T(8,128)(2,1)S(1)} custom-call(s32[8,128]{1,0:T(8,128)} %get-tuple-element.10.plan_ref, f32[1,2432]{1,0:T(1,128)} %get-tuple-element.11.valid_ref, bf16[1536,256]{1,0:T(8,128)(2,1)} %get-tuple-element.12.q_in, bf16[1536,256]{1,0:T(8,128)(2,1)} %get-tuple-element.13.k_in, bf16[1536,256]{1,0:T(8,128)(2,1)} %get-tuple-element.14.v_in), custom_call_target="tpu_custom_call" | custom-call | tf_op jit(solution)/shard_map/bag/pallas_call | solution.py:667
  52.2 0.0 copy-done
  52.2 30.2 %back.1 = bf16[128,2048]{1,0:T(8,128)(2,1)S(1)} custom-call(s32[1]{0:T(128)S(6)} %copy.10.count_ref, s32[8,128]{1,0:T(8,128)S(1)} %bitcast.4, bf16[2,1536,128]{2,1,0:T(8,128)(2,1)S(1)} %bag.1.mixed_ref), custom_call_target="tpu_custom_call" | custom-call | tf_op jit(solution)/shard_map/back/pallas_call | solution.py:682
  82.4 0.8 copy.9
Async XLA Ops:
  43.7 8.6 %copy-start = (s32[1024,1]{0,1:T(1,128)S(1)}, s32[1024,1]{0,1:T(1,128)}, u32[]{:S(2)}) copy-start(s32[1024,1]{0,1:T(1,128)} %param.9) | copy-start | bytes 12292
